TPU v7x, 256 devices: a whole 4x4x8 slice. The times are simulated.
256 devices in a mesh: dp: 32 (over x, z), tensor: 8 (over y, core).
Axes of the slice: x: 4, y: 4, z: 8, core: 2. Of those that a mesh axis runs over, the one named last changes fastest.
Arguments:
- activations: bfloat16 [65536, 4096], P('dp', 'tensor'), may hold values from -6 to 6
- hidden_grads: bfloat16 [65536, 14336], P('dp', 'tensor'), may hold values from -6 to 6
- basis_in: bfloat16 [4096, 64], P('tensor'), may hold values from -0.09375 to 0.09375
- basis_out: bfloat16 [14336, 64], P('tensor'), may hold values from -0.046875 to 0.046875
- precond_out: float32 [64, 64], replicated, may hold values from -0.75 to 0.75
- precond_in: float32 [64, 64], replicated, may hold values from -0.75 to 0.75
- lengths: int32 [128], P('dp'), may hold values from 128 to 512, as said below
- query_ids: int32 [1024], replicated, may hold values from 0 to 127
Outputs:
- scores: float32 [128, 1024], P('dp', 'tensor')
Inputs may be any that keep to these rules, and one draw needn't show every extreme that they name: `lengths`: each block of 4 consecutive examples holds one of length 512.
All inputs are finite; a program needn't handle non-finite values.
Results may differ from a plain program's by a relative error of at most 0.0003.
Values sent between devices are 32-bit elements; how exact they have to be, the bound alone decides.
A program may use at most 64 MiB of HBM per device.

v0:
```python
import jax
import jax.numpy as jnp
from jax import lax
from jax.sharding import PartitionSpec as P


def local(
    activations, hidden_grads, basis_in, basis_out, precond_out, precond_in, lengths, query_ids
):
    examples = lengths.shape[0]
    slots = activations.shape[0] // examples
    rank = basis_in.shape[1]
    queries = query_ids.shape[0]
    tensor_count = lax.axis_size("tensor")
    tensor_index = lax.axis_index("tensor")
    part_act = jnp.dot(activations, basis_in, preferred_element_type=jnp.float32)
    proj_act = lax.psum(part_act, "tensor")
    part_grad = jnp.dot(hidden_grads, basis_out, preferred_element_type=jnp.float32)
    live = (lax.broadcasted_iota(jnp.int32, (examples, slots), 1) < lengths[:, None]).astype(
        jnp.float32
    )
    act_three = proj_act.reshape(examples, slots, rank) * live[:, :, None]
    grad_three = part_grad.reshape(examples, slots, rank)
    part_sketch = jnp.einsum(
        "blr,bls->brs", grad_three, act_three, precision=lax.Precision.HIGHEST
    ) * (1.0 / slots**0.5)
    sketch = lax.psum(part_sketch, "tensor")
    left = jnp.einsum("ij,bjk->bik", precond_out, sketch, precision=lax.Precision.HIGHEST)
    precond = jnp.einsum("bik,kl->bil", left, precond_in, precision=lax.Precision.HIGHEST)
    share = queries // tensor_count
    my_ids = lax.dynamic_slice_in_dim(query_ids, tensor_index * share, share, 0)
    piece = lax.all_gather(sketch, "dp", axis=0, tiled=True)
    columns = lax.broadcasted_iota(jnp.int32, (share, piece.shape[0]), 1)
    onehot = (my_ids[:, None] == columns).astype(jnp.float32)
    chosen = jnp.einsum("qb,bij->qij", onehot, piece, precision=lax.Precision.HIGHEST)
    return jnp.einsum("bij,qij->bq", precond, chosen, precision=lax.Precision.HIGHEST) / rank


def solution(mesh):
    placed = (
        P("dp", "tensor"),
        P("dp", "tensor"),
        P("tensor", None),
        P("tensor", None),
        P(),
        P(),
        P("dp"),
        P(),
    )
    return jax.shard_map(
        local, mesh=mesh, in_specs=placed, out_specs=P("dp", "tensor"), check_vma=False
    )
```

profile of v0, /device:TPU:1, one launch (start us, length us, event | category | flops | bytes accessed | tf_op | source)
XLA Modules:
  0.0 242.9 jit_solution(7731461125401436069)
XLA Ops:
  6.5 0.0 copy-start
  6.5 0.0 copy-start.1
  6.5 0.0 all-reduce.3.cloned.1.call-start
  6.5 1.6 copy-done
  8.1 1.6 fusion.16
  9.7 0.9 copy.26
  10.6 0.0 copy-start.4
  10.6 0.0 all-reduce.3.cloned.1.call-update
  10.6 0.0 copy-start.2
  10.6 0.0 copy-start.3
  10.6 0.0 all-reduce.5.cloned.1.call-start
  10.7 0.0 copy-done.1
  10.7 5.4 %fusion.15 = f32[2048,64]{0,1:T(8,128)S(1)} fusion(bf16[2048,1792]{1,0:T(8,128)(2,1)} %param.9, bf16[1792,64]{0,1:T(8,128)(2,1)S(1)} %copy-done.1), kind=kOutput, calls=%fused_computation.20 | convolution fusion | flops 469762048 | bytes 8093696 | tf_op jit(solution)/shard_map/dot_general | solution.py:18
  16.1 0.0 copy-done.4
  16.1 0.1 fusion.14
  16.1 62.3 %all-reduce.3.cloned.1.call-done = f32[4,512,64]{1,2,0:T(8,128)} async-done(((f32[4,512,64]{1,2,0:T(8,128)}), f32[4,512,64]{1,2,0:T(8,128)}) %all-reduce.3.cloned.1.call-update) | async-done | bytes 524304 | tf_op jit(solution)/shard_map/psum | solution.py:17
  78.4 2.3 convolution_multiply_fusion
  80.8 0.0 all-reduce.5.cloned.1.call-update
  80.8 0.0 all-gather.2.cloned.1.call-start
  80.8 63.7 %all-reduce.5.cloned.1.call-done = f32[4,64,64]{2,1,0:T(8,128)} async-done(((f32[4,64,64]{2,1,0:T(8,128)}), f32[4,64,64]{2,1,0:T(8,128)}) %all-reduce.5.cloned.1.call-update) | async-done | bytes 65552 | tf_op jit(solution)/shard_map/psum | solution.py:27
  144.5 0.0 all-gather.2.cloned.1.call-update
  144.6 0.8 dynamic_slice.3
  145.3 0.0 copy-done.2
  145.3 1.3 convolution_bitcast_fusion
  146.6 0.0 copy-done.3
  146.6 0.4 fusion.10
  147.0 80.4 %all-gather.2.cloned.1.call-done = f32[128,64,64]{2,1,0:T(8,128)} async-done(((f32[4,64,64]{2,1,0:T(8,128)}), f32[128,64,64]{2,1,0:T(8,128)}) %all-gather.2.cloned.1.call-update) | async-done | bytes 2097168 | tf_op jit(solution)/shard_map/all_gather | solution.py:32
  227.4 7.1 %fusion = f32[128,64,64]{0,2,1:T(8,128)S(1)} fusion(f32[128,64,64]{2,1,0:T(8,128)} %all-gather.2.cloned.1.call-done, s32[128]{0:T(128)S(1)} %dynamic_slice.3), kind=kOutput, calls=%fused_computation | convolution fusion | flops 805322752 | bytes 4194816 | tf_op jit(solution)/shard_map/qb,bij->qij/dot_general | solution.py:35
  234.5 1.8 fusion.2
Async XLA Ops:
  6.5 1.6 copy-start
  6.5 4.1 %copy-start.1 = (bf16[1792,64]{0,1:T(8,128)(2,1)S(1)}, bf16[1792,64]{0,1:T(8,128)(2,1)}, u32[]{:S(2)}) copy-start(bf16[1792,64]{0,1:T(8,128)(2,1)} %param.11) | copy-start | bytes 688132
  6.5 71.9 %all-reduce.3.cloned.1.call-start = ((), (), s32[]{:S(2)}) async-start(), calls=%async_computation | async-start | bytes 1048576 | tf_op jit(solution)/shard_map/psum | solution.py:17
  10.6 5.5 %copy-start.4 = (s32[4]{0:T(128)S(1)}, s32[4]{0:T(128)}, u32[]{:S(2)}) copy-start(s32[4]{0:T(128)} %param.14) | copy-start | bytes 52
  10.6 134.8 %copy-start.2 = (f32[64,64]{1,0:T(8,128)S(1)}, f32[64,64]{1,0:T(8,128)}, u32[]{:S(2)}) copy-start(f32[64,64]{1,0:T(8,128)} %param.12) | copy-start | bytes 49156
  10.6 136.0 %copy-start.3 = (f32[64,64]{1,0:T(8,128)S(1)}, f32[64,64]{1,0:T(8,128)}, u32[]{:S(2)}) copy-start(f32[64,64]{1,0:T(8,128)} %param.13) | copy-start | bytes 49156
  10.6 133.9 %all-reduce.5.cloned.1.call-start = ((), (), s32[]{:S(2)}) async-start(), calls=%async_computation.1 | async-start | bytes 262144 | tf_op jit(solution)/shard_map/psum | solution.py:27
  80.8 146.6 %all-gather.2.cloned.1.call-start = ((), (), s32[]{:S(2)}) async-start(), calls=%async_computation.2 | async-start | bytes 4325376 | tf_op jit(solution)/shard_map/all_gather | solution.py:32
Sparse Core Ops, SparseCore 0:
  10.7 67.6 all-reduce.2
  80.9 63.5 all-reduce.4
  147.1 80.2 all-gather.1
where the time goes:
time: 245 us; the launch traced here: 243 us
  waiting for transfers between devices  206 us (84%)
  matrix products  19.9 us (8%)
  between operations  13.2 us (5%)
  local copies, waits for them, and re-layouts  3.22 us (1%)
    all_gather x1, waiting for transfers between devices, local(): piece = lax.all_gather(sketch, 'dp', axis=0, tiled=True)  80.4 us
    psum x1, waiting for transfers between devices, local(): sketch = lax.psum(part_sketch, 'tensor')  63.7 us
    psum x1, waiting for transfers between devices, local(): proj_act = lax.psum(part_act, 'tensor')  62.3 us
    dot_general x1, matrix products, local(): jnp.einsum('qb,bij->qij', onehot, piece, precision=lax.Precision.HIGHEST)  7.11 us
    dot_general x1, matrix products, local(): jnp.dot(hidden_grads, basis_out, preferred_element_type=jnp.float32)  5.39 us
  transfers between devices with their start and end apart: 3, of which 3 were waited for; matrix products, arithmetic and copies ran while one was open for 3% of the time, Pallas kernels for 0%

commit v1 on v0

v1 whole, which is shorter than its diff:
```python
import jax
import jax.numpy as jnp
from jax import lax
from jax.experimental import pallas as pl
from jax.experimental.pallas import tpu as pltpu
from jax.sharding import PartitionSpec as P

MESH = pl.DeviceIdType.MESH
NX, NY, NZ = 4, 4, 8
RANK = 64
OFFSETS = (2, 1, 3, 0)
Z_ARRIVAL = (1, 7, 2, 6, 3, 5, 4)
Z_SEND = (4, 3, 5, 2, 6, 1, 7)
WINDOW = 3
F32 = jnp.float32
BF16 = jnp.bfloat16
NN = (((1,), (0,)), ((), ()))
NT = (((1,), (1,)), ((), ()))
TN = (((0,), (0,)), ((), ()))


def split(value):
    high = value.astype(BF16)
    return high, (value - high.astype(F32)).astype(BF16)


def dot(left, right, dims):
    return lax.dot_general(left, right, dims, preferred_element_type=F32)


def dot_split(left, right, dims):
    left_high, left_low = left
    right_high, right_low = right
    return dot(left_high, right_high, dims) + (
        dot(left_high, right_low, dims) + dot(left_low, right_high, dims)
    )


def kernel(
    act_hbm, grad_hbm, basis_in_hbm, basis_out_hbm, left_hbm, right_hbm, lengths_hbm, ids_hbm,
    out_ref,
    act, grad, basis, left, right, lengths, ids,
    part, pair, gathered, sketch_part, sketch_pair, sketches, preconds, precond_own, score_own, scores,
    load_sem, small_sem, core_send, core_recv, y_send, y_recv, z_send, z_recv, x_send, x_recv,
    p_send, p_recv, f_send, f_recv,
):
    dp = lax.axis_index("dp")
    tensor = lax.axis_index("tensor")
    x, z = dp // NZ, dp % NZ
    y, core = tensor // 2, tensor % 2
    other = 1 - core

    def device(dx, dy, dz, flip):
        to_core = other if flip else core
        return (
            lax.rem(x + dx, NX) * NZ + lax.rem(z + dz, NZ),
            lax.rem(y + dy, NY) * 2 + to_core,
        )

    def remote(src, dst, send, recv, target):
        return pltpu.make_async_remote_copy(
            src_ref=src, dst_ref=dst, send_sem=send, recv_sem=recv,
            device_id=target, device_id_type=MESH,
        )

    half = part.shape[2]
    small = [
        pltpu.make_async_copy(
            basis_in_hbm, basis.at[pl.ds(0, RANK), pl.ds(0, act.shape[1])], small_sem.at[0]
        ),
        pltpu.make_async_copy(
            basis_out_hbm,
            basis.at[pl.ds(RANK, RANK), pl.ds(act.shape[1], grad.shape[1])],
            small_sem.at[1],
        ),
        pltpu.make_async_copy(left_hbm, left, small_sem.at[2]),
        pltpu.make_async_copy(right_hbm, right, small_sem.at[3]),
        pltpu.make_async_copy(lengths_hbm, lengths, small_sem.at[4]),
        pltpu.make_async_copy(ids_hbm, ids, small_sem.at[5]),
    ]

    def rows_of(index):
        step, mine = index // 2, index % 2
        example = lax.rem(y + OFFSETS[step], NY)
        return pl.ds(pl.multiple_of((example * 2 + (core if mine else other)) * half, half), half)

    def loads(index):
        rows = rows_of(index)
        return (
            pltpu.make_async_copy(act_hbm.at[rows], act.at[rows], load_sem.at[0, index]),
            pltpu.make_async_copy(grad_hbm.at[rows], grad.at[rows], load_sem.at[1, index]),
        )

    small[0].start()
    small[1].start()
    for index in range(WINDOW):
        for copy in loads(index):
            copy.start()
    for copy in small[2:]:
        copy.start()

    barrier = pltpu.get_barrier_semaphore()
    partners = [(0, dy, 0, flip) for dy in range(NY) for flip in (0, 1) if dy or flip]
    partners += [(0, 0, dz, 0) for dz in range(1, NZ)]
    partners += [(dx, 0, 0, 0) for dx in range(1, NX)]
    for partner in partners:
        pl.semaphore_signal(barrier, 1, device_id=device(*partner), device_id_type=MESH)

    basis[0:RANK, act.shape[1] :] = jnp.zeros((RANK, grad.shape[1]), BF16)
    basis[RANK:, 0 : act.shape[1]] = jnp.zeros((RANK, act.shape[1]), BF16)
    small[0].wait()
    small[1].wait()

    def project(index):
        for copy in loads(index):
            copy.wait()
        if index + WINDOW < 2 * len(OFFSETS):
            for copy in loads(index + WINDOW):
                copy.start()
        rows = rows_of(index)
        part[index // 2, index % 2] = dot(act[rows, :], basis[:, 0 : act.shape[1]], NT) + dot(
            grad[rows, :], basis[:, act.shape[1] :], NT
        )

    def to_core(step):
        return remote(
            part.at[step, 0], pair.at[step], core_send.at[step], core_recv.at[step],
            device(0, 0, 0, 1),
        )

    def to_chip(step):
        return remote(
            part.at[step, 1], gathered.at[step], y_send.at[step], y_recv.at[step],
            device(0, OFFSETS[step], 0, 0),
        )

    def merge(step):
        to_core(step).wait_recv()
        part[step, 1] = part[step, 1] + pair[step]
        if OFFSETS[step]:
            to_chip(step).start()

    for step in range(len(OFFSETS)):
        project(2 * step)
        if step == 0:
            pl.semaphore_wait(barrier, len(partners))
        to_core(step).start()
        project(2 * step + 1)
        if step:
            merge(step - 1)
    merge(len(OFFSETS) - 1)

    last = len(OFFSETS) - 1
    for copy in small[2:]:
        copy.wait()
    left_split = split(left[...])
    right_split = split(right[...])
    total = part[last, 1]
    for step in range(last):
        to_chip(step).wait_recv()
        total = total + gathered[step]
    slot = lax.broadcasted_iota(jnp.int32, total.shape, 0) + core * half
    total = jnp.where(slot < lengths[y], total, 0.0)
    total_split = split(total)
    square = dot_split(total_split, total_split, TN)
    corner = square[RANK:, 0:RANK]
    sketch_part[...] = jnp.concatenate([corner[: RANK // 2], corner[RANK // 2 :]], axis=1)
    swap = remote(
        sketch_part, sketch_pair, core_send.at[last + 1], core_recv.at[last + 1],
        device(0, 0, 0, 1),
    )
    swap.start()
    swap.wait_recv()
    packed = sketch_part[...] + sketch_pair[...]
    sketch_pair[...] = packed

    block = RANK // 4

    def place(at_x, at_z):
        return sketches.at[pl.ds(pl.multiple_of((at_x * NZ + at_z) * block, block), block)]

    own_rows = pl.ds(pl.multiple_of(core * block, block), block)
    sketches[pl.ds(pl.multiple_of((x * NZ + z) * block, block), block), :] = sketch_pair[own_rows, :]
    own = place(x, z)

    def to_z(dz):
        return remote(own, own, z_send.at[dz], z_recv.at[dz], device(0, 0, dz, 0))

    def from_z(dz):
        spot = place(x, lax.rem(z + NZ - dz, NZ))
        return remote(spot, spot, z_send.at[dz], z_recv.at[dz], device(0, 0, dz, 0))

    def to_x(dx, dz):
        spot = place(x, lax.rem(z + NZ - dz, NZ))
        return remote(spot, spot, x_send.at[dx, dz], x_recv.at[dx, dz], device(dx, 0, 0, 0))

    def from_x(dx, dz):
        spot = place(lax.rem(x + NX - dx, NX), lax.rem(z + NZ - dz, NZ))
        return remote(spot, spot, x_send.at[dx, dz], x_recv.at[dx, dz], device(dx, 0, 0, 0))

    for dz in Z_SEND:
        to_z(dz).start()
    for dx in (2, 1, 3):
        to_x(dx, 0).start()

    whole = jnp.concatenate([packed[:, 0:RANK], packed[:, RANK:]], axis=0)
    halfway = dot_split(split(whole), right_split, NN)
    precond = dot_split(left_split, split(halfway), NN)
    precond_own[...] = jnp.concatenate([precond[: RANK // 2], precond[RANK // 2 :]], axis=1)

    def p_place(at_y):
        return preconds.at[pl.ds(pl.multiple_of(at_y * block, block), block)]

    preconds[pl.ds(pl.multiple_of(y * block, block), block), :] = precond_own[own_rows, :]

    def to_y(dy):
        return remote(p_place(y), p_place(y), p_send.at[dy], p_recv.at[dy], device(0, dy, 0, 0))

    def from_y(dy):
        spot = p_place(lax.rem(y + NY - dy, NY))
        return remote(spot, spot, p_send.at[dy], p_recv.at[dy], device(0, dy, 0, 0))

    for dy in (2, 1, 3):
        to_y(dy).start()

    for dz in Z_ARRIVAL:
        from_z(dz).wait_recv()
        for dx in (2, 1, 3):
            to_x(dx, dz).start()
    for dy in range(1, NY):
        from_y(dy).wait_recv()
    weights = split(
        jnp.concatenate([preconds[pl.ds(row, NY, stride=block), :] for row in range(block)], axis=1)
    )
    for dz in (0,) + Z_ARRIVAL:
        for dx in (1, 3, 2):
            from_x(dx, dz).wait_recv()
    rows = NX * NZ
    found = split(
        jnp.concatenate([sketches[pl.ds(row, rows, stride=block), :] for row in range(block)], axis=1)
    )
    found = [jnp.concatenate([term] * NY, axis=0) for term in found]
    lane = lax.broadcasted_iota(jnp.int32, (NY, rows * NY), 1)
    mine = jnp.where(lane // rows == y, dot_split(weights, found, NT), 0.0)

    score_own[0:NY, :] = mine
    score_own[NY:, :] = jnp.zeros((8 - NY, rows * NY), F32)

    def exchange(dy, flip):
        index = dy * 2 + flip
        return remote(
            score_own, scores.at[index], f_send.at[index], f_recv.at[index], device(0, dy, 0, flip)
        )

    everyone = [(dy, flip) for dy in (2, 1, 3, 0) for flip in (1, 0) if dy or flip]
    for pair_to in everyone:
        exchange(*pair_to).start()
    query = ids[pl.ds(tensor, 1), :]
    spot = lax.broadcasted_iota(jnp.int32, (rows * NY, rows * NY), 0)
    onehot = jnp.where(spot % rows * NY + spot // rows == query, 1.0, 0.0).astype(BF16)
    table = score_own[...]
    for pair_to in everyone[::-1]:
        exchange(*pair_to).wait_recv()
    for pair_to in everyone:
        table = table + scores[pair_to[0] * 2 + pair_to[1]]
    high, low = split(table)
    lowest = (table - high.astype(F32) - low.astype(F32)).astype(BF16)
    picked = dot(high, onehot, NN) + (dot(low, onehot, NN) + dot(lowest, onehot, NN))
    out_ref[...] = picked[0:NY, :] * (1.0 / (2 * half * RANK))

    for step in range(len(OFFSETS)):
        to_core(step).wait_send()
        if OFFSETS[step]:
            to_chip(step).wait_send()
    swap.wait_send()
    for dz in Z_SEND:
        to_z(dz).wait_send()
    for dz in range(NZ):
        for dx in range(1, NX):
            to_x(dx, dz).wait_send()
    for dy in range(1, NY):
        to_y(dy).wait_send()
    for pair_to in everyone:
        exchange(*pair_to).wait_send()


def local(
    activations, hidden_grads, basis_in, basis_out, precond_out, precond_in, lengths, query_ids
):
    tokens, features = activations.shape
    hidden = hidden_grads.shape[1]
    half = tokens // (2 * NY)
    dma = pltpu.SemaphoreType.DMA
    return pl.pallas_call(
        kernel,
        out_shape=jax.ShapeDtypeStruct((NY, query_ids.shape[0] // (2 * NY)), F32),
        in_specs=[pl.BlockSpec(memory_space=pltpu.HBM)] * 8,
        out_specs=pl.BlockSpec(memory_space=pltpu.VMEM),
        scratch_shapes=[
            pltpu.VMEM((tokens, features), BF16),
            pltpu.VMEM((tokens, hidden), BF16),
            pltpu.VMEM((2 * RANK, features + hidden), BF16),
            pltpu.VMEM((RANK, RANK), F32),
            pltpu.VMEM((RANK, RANK), F32),
            pltpu.SMEM((NY,), jnp.int32),
            pltpu.VMEM((2 * NY, query_ids.shape[0] // (2 * NY)), jnp.int32),
            pltpu.VMEM((NY, 2, half, 2 * RANK), F32),
            pltpu.VMEM((NY, half, 2 * RANK), F32),
            pltpu.VMEM((NY - 1, half, 2 * RANK), F32),
            pltpu.VMEM((RANK // 2, 2 * RANK), F32),
            pltpu.VMEM((RANK // 2, 2 * RANK), F32),
            pltpu.VMEM((NX * NZ * RANK // 4, 2 * RANK), F32),
            pltpu.VMEM((NY * RANK // 4, 2 * RANK), F32),
            pltpu.VMEM((RANK // 2, 2 * RANK), F32),
            pltpu.VMEM((8, 2 * RANK), F32),
            pltpu.VMEM((8, 8, 2 * RANK), F32),
            dma((2, 2 * NY)),
            dma((6,)),
            dma((NY + 1,)),
            dma((NY + 1,)),
            dma((NY,)),
            dma((NY,)),
            dma((NZ,)),
            dma((NZ,)),
            dma((NX, NZ)),
            dma((NX, NZ)),
            dma((NY,)),
            dma((NY,)),
            dma((2 * NY,)),
            dma((2 * NY,)),
        ],
        compiler_params=pltpu.CompilerParams(
            collective_id=0, has_side_effects=True, vmem_limit_bytes=60 * 2**20
        ),
        name="sketch_scores",
    )(
        activations, hidden_grads, basis_in.T, basis_out.T, precond_out, precond_in, lengths,
        query_ids.reshape(2 * NY, -1),
    )


def solution(mesh):
    placed = (
        P("dp", "tensor"),
        P("dp", "tensor"),
        P("tensor", None),
        P("tensor", None),
        P(),
        P(),
        P("dp"),
        P(),
    )
    return jax.shard_map(
        local, mesh=mesh, in_specs=placed, out_specs=P("dp", "tensor"), check_vma=False
    )
```

time: 245 us -> 37.9 us (0.15)
  waiting for transfers between devices: 206 us -> 0 us
  Pallas kernels: 0 us -> 36.5 us
  matrix products: 19.9 us -> 0 us
  between operations: 13.2 us -> 0.01 us
    psum x2 -> x0, waiting for transfers between devices: 126 us -> none  [the longest x1 63.7 us: local(): sketch = lax.psum(part_sketch, 'tensor')]
    all_gather x1 -> x0, waiting for transfers between devices: 80.4 us -> none  [local(): piece = lax.all_gather(sketch, 'dp', axis=0, tiled=True)]
    pallas_call x0 -> x1, Pallas kernels: none -> 36.5 us  [local(): pl.pallas_call(kernel, out_shape=jax.ShapeDtypeStruct((NY, query_ids.shap...]
    dot_general x7 -> x0, matrix products: 19.9 us -> none  [the longest x1 7.11 us: local(): jnp.einsum('qb,bij->qij', onehot, piece, precision=lax.Precision.HIGHEST)]
  transfers between devices with their start and end apart: 3 -> 0, of which waited for: 3 -> 0; matrix products, arithmetic and copies ran while one was open for 3% -> 0% of each run, Pallas kernels for 0% -> 0%
where the time goes in v1:
time: 37.9 us; the launch traced here: 37.8 us
  Pallas kernels  36.5 us (96%)
  local copies, waits for them, and re-layouts  1.26 us (3%)
    pallas_call x1, Pallas kernels, local(): pl.pallas_call(kernel, out_shape=jax.ShapeDtypeStruct((NY, query_ids.shap...  36.5 us
    unnamed x1, local copies, waits for them, and re-layouts  1.26 us

profile of v1, /device:TPU:1, one launch (start us, length us, event | category | flops | bytes accessed | tf_op | source)
XLA Modules:
  0.0 37.8 jit_solution(10187638565333651557)
XLA Ops:
  0.0 36.5 %sketch_scores.1 = f32[4,128]{1,0:T(4,128)} custom-call(bf16[2048,512]{1,0:T(8,128)(2,1)} %act_hbm.1, bf16[2048,1792]{1,0:T(8,128)(2,1)} %grad_hbm.1, bf16[64,512]{1,0:T(8,128)(2,1)} %bitcast.4, bf16[64,1792]{1,0:T(8,128)(2,1)} %bitcast.3, f32[64,64]{1,0:T(8,128)} %left_hbm.1, f32[64,64]{1,0:T(8,128)} %right_hbm.1, s32[4]{0:T(128)} %lengths_hbm.1, ...), custom_call_target="tpu_custom_call" | custom-call | tf_op jit(solution)/shard_map/sketch_scores/pallas_call | solution.py:294
  36.5 1.3 %copy.10 = f32[4,128]{1,0:T(4,128)} copy(f32[4,128]{1,0:T(4,128)} %sketch_scores.1) | data formatting | bytes 4096

commit v2 on v1

v2 whole, which is shorter than its diff:
```python
import jax
import jax.numpy as jnp
from jax import lax
from jax.experimental import pallas as pl
from jax.experimental.pallas import tpu as pltpu
from jax.sharding import PartitionSpec as P

MESH = pl.DeviceIdType.MESH
NX, NY, NZ = 4, 4, 8
RANK = 64
OFFSETS = (2, 1, 3, 0)
Z_ARRIVAL = (1, 7, 2, 6, 3, 5, 4)
Z_SEND = (4, 3, 5, 2, 6, 1, 7)
ORDER = ((0, 0), (0, 1), (1, 0), (2, 0), (1, 1), (2, 1), (3, 0), (3, 1))
MERGES = {3: 0, 4: 1, 5: 2, 7: 3}
WINDOW = 5
F32 = jnp.float32
BF16 = jnp.bfloat16
NN = (((1,), (0,)), ((), ()))
NT = (((1,), (1,)), ((), ()))
TN = (((0,), (0,)), ((), ()))


def split(value):
    high = value.astype(BF16)
    return high, (value - high.astype(F32)).astype(BF16)


def dot(left, right, dims):
    return lax.dot_general(left, right, dims, preferred_element_type=F32)


def dot_split(left, right, dims):
    left_high, left_low = left
    right_high, right_low = right
    return dot(left_high, right_high, dims) + (
        dot(left_high, right_low, dims) + dot(left_low, right_high, dims)
    )


def kernel(
    act_hbm, grad_hbm, basis_in_hbm, basis_out_hbm, left_hbm, right_hbm, lengths_hbm, ids_hbm,
    out_ref,
    act, grad, basis, weight, factors, lengths, ids,
    part, pair, gathered, sketch_part, sketch_pair, sketches, preconds, precond_own, score_own, scores,
    load_sem, small_sem, core_send, core_recv, swap_sem, y_send, y_recv, z_send, z_recv, x_send, x_recv,
    p_sem, f_sem,
):
    dp = lax.axis_index("dp")
    tensor = lax.axis_index("tensor")
    x, z = dp // NZ, dp % NZ
    y, core = tensor // 2, tensor % 2
    other = 1 - core

    def device(dx, dy, dz, flip):
        to_core = other if flip else core
        return (
            lax.rem(x + dx, NX) * NZ + lax.rem(z + dz, NZ),
            lax.rem(y + dy, NY) * 2 + to_core,
        )

    def remote(src, dst, send, recv, target):
        return pltpu.make_async_remote_copy(
            src_ref=src, dst_ref=dst, send_sem=send, recv_sem=recv,
            device_id=target, device_id_type=MESH,
        )

    def take(ref, sem):
        pltpu.make_async_copy(ref, ref, sem).wait()

    half = part.shape[2]
    small = [
        pltpu.make_async_copy(
            basis_in_hbm, basis.at[pl.ds(0, RANK), pl.ds(0, act.shape[1])], small_sem.at[0]
        ),
        pltpu.make_async_copy(
            basis_out_hbm,
            basis.at[pl.ds(RANK, RANK), pl.ds(act.shape[1], grad.shape[1])],
            small_sem.at[0],
        ),
        pltpu.make_async_copy(left_hbm, factors.at[pl.ds(0, RANK)], small_sem.at[1]),
        pltpu.make_async_copy(right_hbm, factors.at[pl.ds(RANK, RANK)], small_sem.at[1]),
        pltpu.make_async_copy(lengths_hbm, lengths, small_sem.at[2]),
        pltpu.make_async_copy(ids_hbm, ids, small_sem.at[3]),
    ]

    def load(index):
        step, mine = ORDER[index]
        example = lax.rem(y + OFFSETS[step], NY)
        rows = pl.ds(pl.multiple_of((example * 2 + (core if mine else other)) * half, half), half)
        slot = pl.ds(index * half, half)
        pltpu.make_async_copy(act_hbm.at[rows], act.at[slot], load_sem.at[index]).start()
        pltpu.make_async_copy(grad_hbm.at[rows], grad.at[slot], load_sem.at[index]).start()

    small[0].start()
    small[1].start()
    load(0)

    barrier = pltpu.get_barrier_semaphore()
    partners = [(0, dy, 0, flip) for dy in range(NY) for flip in (0, 1) if dy or flip]
    partners += [(0, 0, dz, 0) for dz in range(1, NZ)]
    partners += [(dx, 0, 0, 0) for dx in range(1, NX)]
    for partner in partners:
        pl.semaphore_signal(barrier, 1, device_id=device(*partner), device_id_type=MESH)

    load(1)
    basis[0:RANK, act.shape[1] :] = jnp.zeros((RANK, grad.shape[1]), BF16)
    basis[RANK:, 0 : act.shape[1]] = jnp.zeros((RANK, act.shape[1]), BF16)
    take(basis.at[pl.ds(0, RANK)], small_sem.at[0])
    for index in range(2, WINDOW):
        load(index)
    for copy in small[2:]:
        copy.start()
    weight[...] = basis[...].T

    def project(index):
        step, mine = ORDER[index]
        take(act.at[pl.ds(0, half * (act.shape[1] + grad.shape[1]) // act.shape[1])], load_sem.at[index])
        if index + WINDOW < len(ORDER):
            load(index + WINDOW)
        slot = pl.ds(index * half, half)
        part[step, mine] = dot(act[slot, :], weight[0 : act.shape[1], :], NN) + dot(
            grad[slot, :], weight[act.shape[1] :, :], NN
        )
        if not mine:
            if index == 0:
                pl.semaphore_wait(barrier, len(partners))
            to_core(step).start()

    def to_core(step):
        return remote(
            part.at[step, 0], pair.at[step], core_send, core_recv.at[step],
            device(0, 0, 0, 1),
        )

    def to_chip(step):
        return remote(
            part.at[step, 1], gathered.at[step], y_send, y_recv.at[step],
            device(0, OFFSETS[step], 0, 0),
        )

    def merge(step):
        to_core(step).wait_recv()
        part[step, 1] = part[step, 1] + pair[step]
        if OFFSETS[step]:
            to_chip(step).start()

    for index in range(len(ORDER)):
        project(index)
        if index in MERGES:
            merge(MERGES[index])

    last = len(OFFSETS) - 1
    take(factors, small_sem.at[1])
    for copy in small[4:]:
        copy.wait()
    left_split = split(factors[0:RANK, :])
    right_split = split(factors[RANK:, :])
    total = part[last, 1]
    for step in range(last):
        to_chip(step).wait_recv()
        total = total + gathered[step]
    slot = lax.broadcasted_iota(jnp.int32, total.shape, 0) + core * half
    total = jnp.where(slot < lengths[y], total, 0.0)
    total_split = split(total)
    square = dot_split(total_split, total_split, TN)
    corner = square[RANK:, 0:RANK]
    sketch_part[...] = jnp.concatenate([corner[: RANK // 2], corner[RANK // 2 :]], axis=1)
    swap = remote(
        sketch_part, sketch_pair, swap_sem.at[0], swap_sem.at[1],
        device(0, 0, 0, 1),
    )
    swap.start()
    swap.wait_recv()
    packed = sketch_part[...] + sketch_pair[...]
    sketch_pair[...] = packed

    block = RANK // 4

    def place(at_x, at_z):
        return sketches.at[pl.ds(pl.multiple_of((at_x * NZ + at_z) * block, block), block)]

    own_rows = pl.ds(pl.multiple_of(core * block, block), block)
    sketches[pl.ds(pl.multiple_of((x * NZ + z) * block, block), block), :] = sketch_pair[own_rows, :]
    own = place(x, z)

    def to_z(dz):
        return remote(own, own, z_send, z_recv.at[dz], device(0, 0, dz, 0))

    def from_z(dz):
        spot = place(x, lax.rem(z + NZ - dz, NZ))
        return remote(spot, spot, z_send, z_recv.at[dz], device(0, 0, dz, 0))

    def to_x(dx, dz):
        spot = place(x, lax.rem(z + NZ - dz, NZ))
        return remote(spot, spot, x_send, x_recv.at[dx], device(dx, 0, 0, 0))

    for dz in Z_SEND:
        to_z(dz).start()
    for dx in (2, 1, 3):
        to_x(dx, 0).start()

    whole = jnp.concatenate([packed[:, 0:RANK], packed[:, RANK:]], axis=0)
    halfway = dot_split(split(whole), right_split, NN)
    precond = dot_split(left_split, split(halfway), NN)
    precond_own[...] = jnp.concatenate([precond[: RANK // 2], precond[RANK // 2 :]], axis=1)

    def p_place(at_y):
        return preconds.at[pl.ds(pl.multiple_of(at_y * block, block), block)]

    preconds[pl.ds(pl.multiple_of(y * block, block), block), :] = precond_own[own_rows, :]

    def to_y(dy):
        return remote(p_place(y), p_place(y), p_sem.at[0], p_sem.at[1], device(0, dy, 0, 0))

    for dy in (2, 1, 3):
        to_y(dy).start()

    for dz in Z_ARRIVAL:
        from_z(dz).wait_recv()
        for dx in (2, 1, 3):
            to_x(dx, dz).start()
    take(preconds.at[pl.ds(0, (NY - 1) * block)], p_sem.at[1])
    weights = split(
        jnp.concatenate([preconds[pl.ds(row, NY, stride=block), :] for row in range(block)], axis=1)
    )
    for dx in (1, 3, 2):
        take(sketches.at[pl.ds(0, NZ * block)], x_recv.at[dx])
    rows = NX * NZ
    found = split(
        jnp.concatenate([sketches[pl.ds(row, rows, stride=block), :] for row in range(block)], axis=1)
    )
    found = [jnp.concatenate([term] * NY, axis=0) for term in found]
    lane = lax.broadcasted_iota(jnp.int32, (NY, rows * NY), 1)
    mine = jnp.where(lane // rows == y, dot_split(weights, found, NT), 0.0)

    score_own[0:NY, :] = mine
    score_own[NY:, :] = jnp.zeros((8 - NY, rows * NY), F32)

    def exchange(dy, flip):
        index = dy * 2 + flip
        return remote(
            score_own, scores.at[index], f_sem.at[0], f_sem.at[1], device(0, dy, 0, flip)
        )

    everyone = [(dy, flip) for dy in (2, 1, 3, 0) for flip in (1, 0) if dy or flip]
    for pair_to in everyone:
        exchange(*pair_to).start()
    query = ids[pl.ds(tensor, 1), :]
    spot = lax.broadcasted_iota(jnp.int32, (rows * NY, rows * NY), 0)
    onehot = jnp.where(spot % rows * NY + spot // rows == query, 1.0, 0.0).astype(BF16)
    table = score_own[...]
    take(scores.at[pl.ds(0, len(everyone))], f_sem.at[1])
    for pair_to in everyone:
        table = table + scores[pair_to[0] * 2 + pair_to[1]]
    high, low = split(table)
    lowest = (table - high.astype(F32) - low.astype(F32)).astype(BF16)
    picked = dot(high, onehot, NN) + (dot(low, onehot, NN) + dot(lowest, onehot, NN))
    out_ref[...] = picked[0:NY, :] * (1.0 / (2 * half * RANK))

    take(part.at[pl.ds(0, NY // 2)], core_send)
    take(gathered, y_send)
    take(sketch_part, swap_sem.at[0])
    take(sketches.at[pl.ds(0, (NZ - 1) * block)], z_send)
    take(sketches.at[pl.ds(0, (NX - 1) * NZ * block)], x_send)
    take(preconds.at[pl.ds(0, (NY - 1) * block)], p_sem.at[0])
    take(scores.at[pl.ds(0, len(everyone))], f_sem.at[0])


def local(
    activations, hidden_grads, basis_in, basis_out, precond_out, precond_in, lengths, query_ids
):
    tokens, features = activations.shape
    hidden = hidden_grads.shape[1]
    half = tokens // (2 * NY)
    dma = pltpu.SemaphoreType.DMA
    return pl.pallas_call(
        kernel,
        out_shape=jax.ShapeDtypeStruct((NY, query_ids.shape[0] // (2 * NY)), F32),
        in_specs=[pl.BlockSpec(memory_space=pltpu.HBM)] * 8,
        out_specs=pl.BlockSpec(memory_space=pltpu.VMEM),
        scratch_shapes=[
            pltpu.VMEM((tokens, features), BF16),
            pltpu.VMEM((tokens, hidden), BF16),
            pltpu.VMEM((2 * RANK, features + hidden), BF16),
            pltpu.VMEM((features + hidden, 2 * RANK), BF16),
            pltpu.VMEM((2 * RANK, RANK), F32),
            pltpu.SMEM((NY,), jnp.int32),
            pltpu.VMEM((2 * NY, query_ids.shape[0] // (2 * NY)), jnp.int32),
            pltpu.VMEM((NY, 2, half, 2 * RANK), F32),
            pltpu.VMEM((NY, half, 2 * RANK), F32),
            pltpu.VMEM((NY - 1, half, 2 * RANK), F32),
            pltpu.VMEM((RANK // 2, 2 * RANK), F32),
            pltpu.VMEM((RANK // 2, 2 * RANK), F32),
            pltpu.VMEM((NX * NZ * RANK // 4, 2 * RANK), F32),
            pltpu.VMEM((NY * RANK // 4, 2 * RANK), F32),
            pltpu.VMEM((RANK // 2, 2 * RANK), F32),
            pltpu.VMEM((8, 2 * RANK), F32),
            pltpu.VMEM((8, 8, 2 * RANK), F32),
            dma((len(ORDER),)),
            dma((4,)),
            dma(()),
            dma((NY,)),
            dma((2,)),
            dma(()),
            dma((NY - 1,)),
            dma(()),
            dma((NZ,)),
            dma(()),
            dma((NX,)),
            dma((2,)),
            dma((2,)),
        ],
        compiler_params=pltpu.CompilerParams(
            collective_id=0, has_side_effects=True, vmem_limit_bytes=60 * 2**20
        ),
        name="sketch_scores",
    )(
        activations, hidden_grads, basis_in.T, basis_out.T, precond_out, precond_in, lengths,
        query_ids.reshape(2 * NY, -1),
    )


def solution(mesh):
    placed = (
        P("dp", "tensor"),
        P("dp", "tensor"),
        P("tensor", None),
        P("tensor", None),
        P(),
        P(),
        P("dp"),
        P(),
    )
    return jax.shard_map(
        local, mesh=mesh, in_specs=placed, out_specs=P("dp", "tensor"), check_vma=False
    )
```

time: 37.9 us -> 35.9 us (0.947)
  Pallas kernels: 36.5 us -> 34.5 us
    pallas_call x1, Pallas kernels: 36.5 us -> 34.5 us  [local(): pl.pallas_call(kernel, out_shape=jax.ShapeDtypeStruct((NY, query_ids.shap...]
where the time goes in v2:
time: 35.9 us; the launch traced here: 35.8 us
  Pallas kernels  34.5 us (96%)
  local copies, waits for them, and re-layouts  1.26 us (4%)
    pallas_call x1, Pallas kernels, local(): pl.pallas_call(kernel, out_shape=jax.ShapeDtypeStruct((NY, query_ids.shap...  34.5 us
    unnamed x1, local copies, waits for them, and re-layouts  1.26 us

profile of v2, /device:TPU:1, one launch (start us, length us, event | category | flops | bytes accessed | tf_op | source)
XLA Modules:
  0.0 35.8 jit_solution(17438705030135346778)
XLA Ops:
  0.0 34.5 %sketch_scores.1 = f32[4,128]{1,0:T(4,128)} custom-call(bf16[2048,512]{1,0:T(8,128)(2,1)} %act_hbm.1, bf16[2048,1792]{1,0:T(8,128)(2,1)} %grad_hbm.1, bf16[64,512]{1,0:T(8,128)(2,1)} %bitcast.4, bf16[64,1792]{1,0:T(8,128)(2,1)} %bitcast.3, f32[64,64]{1,0:T(8,128)} %left_hbm.1, f32[64,64]{1,0:T(8,128)} %right_hbm.1, s32[4]{0:T(128)} %lengths_hbm.1, ...), custom_call_target="tpu_custom_call" | custom-call | tf_op jit(solution)/shard_map/sketch_scores/pallas_call | solution.py:277
  34.5 1.3 %copy.10 = f32[4,128]{1,0:T(4,128)} copy(f32[4,128]{1,0:T(4,128)} %sketch_scores.1) | data formatting | bytes 4096

commit v3 on v2

--- a/solution.py
+++ b/solution.py
@@ -10,9 +10,8 @@
 RANK = 64
 OFFSETS = (2, 1, 3, 0)
 Z_ARRIVAL = (1, 7, 2, 6, 3, 5, 4)
-Z_SEND = (4, 3, 5, 2, 6, 1, 7)
 ORDER = ((0, 0), (0, 1), (1, 0), (2, 0), (1, 1), (2, 1), (3, 0), (3, 1))
-MERGES = {3: 0, 4: 1, 5: 2, 7: 3}
+MERGES = {2: 0, 4: 1, 5: 2}
 WINDOW = 5
 F32 = jnp.float32
 BF16 = jnp.bfloat16
@@ -42,8 +41,8 @@
     act_hbm, grad_hbm, basis_in_hbm, basis_out_hbm, left_hbm, right_hbm, lengths_hbm, ids_hbm,
     out_ref,
     act, grad, basis, weight, factors, lengths, ids,
-    part, pair, gathered, sketch_part, sketch_pair, sketches, preconds, precond_own, score_own, scores,
-    load_sem, small_sem, core_send, core_recv, swap_sem, y_send, y_recv, z_send, z_recv, x_send, x_recv,
+    part, pair, relayed, gathered, sketch_part, sketch_pair, sketches, preconds, precond_own, score_own, scores,
+    load_sem, small_sem, core_send, core_recv, swap_sem, relay_send, relay_recv, y_send, y_recv, z_send, z_recv, x_send, x_recv,
     p_sem, f_sem,
 ):
     dp = lax.axis_index("dp")
@@ -51,6 +50,12 @@
     x, z = dp // NZ, dp % NZ
     y, core = tensor // 2, tensor % 2
     other = 1 - core
+
+    def others(here, size):
+        return [
+            lax.rem(there + (there >= here).astype(jnp.int32) - here + size, size)
+            for there in range(size - 1)
+        ]
 
     def device(dx, dy, dz, flip):
         to_core = other if flip else core
@@ -133,22 +138,44 @@
             device(0, 0, 0, 1),
         )
 
-    def to_chip(step):
+    quarter = half // 2
+
+    def to_relay(up):
+        piece = pl.ds(0 if up else quarter, quarter)
         return remote(
-            part.at[step, 1], gathered.at[step], y_send, y_recv.at[step],
-            device(0, OFFSETS[step], 0, 0),
+            part.at[0, 1, piece], relayed.at[up], relay_send, relay_recv.at[up],
+            device(0, 1 if up else NY - 1, 0, 0),
+        )
+
+    def to_chip(up, first):
+        piece = pl.ds(0 if first else quarter, quarter)
+        return remote(
+            part.at[2 - up, 1, piece], gathered.at[up, piece], y_send, y_recv.at[up],
+            device(0, 1 if up else NY - 1, 0, 0),
         )
 
     def merge(step):
         to_core(step).wait_recv()
         part[step, 1] = part[step, 1] + pair[step]
-        if OFFSETS[step]:
-            to_chip(step).start()
+        if step == 0:
+            to_relay(1).start()
+            to_relay(0).start()
+        elif step < 3:
+            to_chip(2 - step, step == 2).start()
+
+    def relay(up):
+        piece = slice(0, quarter) if up else slice(quarter, half)
+        to_relay(up).wait_recv()
+        part[2 - up, 1, piece] = part[2 - up, 1, piece] + relayed[up]
+        to_chip(up, up == 1).start()
 
     for index in range(len(ORDER)):
         project(index)
         if index in MERGES:
             merge(MERGES[index])
+    relay(1)
+    relay(0)
+    merge(3)
 
     last = len(OFFSETS) - 1
     take(factors, small_sem.at[1])
@@ -157,9 +184,9 @@
     left_split = split(factors[0:RANK, :])
     right_split = split(factors[RANK:, :])
     total = part[last, 1]
-    for step in range(last):
-        to_chip(step).wait_recv()
-        total = total + gathered[step]
+    for up in (1, 0):
+        take(gathered.at[up], y_recv.at[up])
+        total = total + gathered[up]
     slot = lax.broadcasted_iota(jnp.int32, total.shape, 0) + core * half
     total = jnp.where(slot < lengths[y], total, 0.0)
     total_split = split(total)
@@ -195,9 +222,9 @@
         spot = place(x, lax.rem(z + NZ - dz, NZ))
         return remote(spot, spot, x_send, x_recv.at[dx], device(dx, 0, 0, 0))
 
-    for dz in Z_SEND:
+    for dz in others(z, NZ):
         to_z(dz).start()
-    for dx in (2, 1, 3):
+    for dx in others(x, NX):
         to_x(dx, 0).start()
 
     whole = jnp.concatenate([packed[:, 0:RANK], packed[:, RANK:]], axis=0)
@@ -213,12 +240,12 @@
     def to_y(dy):
         return remote(p_place(y), p_place(y), p_sem.at[0], p_sem.at[1], device(0, dy, 0, 0))
 
-    for dy in (2, 1, 3):
+    for dy in others(y, NY):
         to_y(dy).start()
 
     for dz in Z_ARRIVAL:
         from_z(dz).wait_recv()
-        for dx in (2, 1, 3):
+        for dx in others(x, NX):
             to_x(dx, dz).start()
     take(preconds.at[pl.ds(0, (NY - 1) * block)], p_sem.at[1])
     weights = split(
@@ -230,41 +257,37 @@
     found = split(
         jnp.concatenate([sketches[pl.ds(row, rows, stride=block), :] for row in range(block)], axis=1)
     )
-    found = [jnp.concatenate([term] * NY, axis=0) for term in found]
-    lane = lax.broadcasted_iota(jnp.int32, (NY, rows * NY), 1)
-    mine = jnp.where(lane // rows == y, dot_split(weights, found, NT), 0.0)
-
-    score_own[0:NY, :] = mine
-    score_own[NY:, :] = jnp.zeros((8 - NY, rows * NY), F32)
-
-    def exchange(dy, flip):
-        index = dy * 2 + flip
-        return remote(
-            score_own, scores.at[index], f_sem.at[0], f_sem.at[1], device(0, dy, 0, flip)
-        )
-
-    everyone = [(dy, flip) for dy in (2, 1, 3, 0) for flip in (1, 0) if dy or flip]
-    for pair_to in everyone:
-        exchange(*pair_to).start()
+    mine = dot_split(weights, found, NT)
+    mine = jnp.concatenate([mine, jnp.zeros((NY, rows * (NY - 1)), F32)], axis=1)
+    mine = jnp.concatenate([mine, jnp.zeros((8 - NY, rows * NY), F32)], axis=0)
+    mine = pltpu.roll(mine, y * rows, 1)
+
+    score_own[...] = mine
+
+    def exchange(change):
+        target = lax.rem(tensor + change, 2 * NY)
+        return remote(score_own, scores.at[change], f_sem.at[0], f_sem.at[1], (dp, target))
+
+    for change in others(tensor, 2 * NY):
+        exchange(change).start()
     query = ids[pl.ds(tensor, 1), :]
     spot = lax.broadcasted_iota(jnp.int32, (rows * NY, rows * NY), 0)
     onehot = jnp.where(spot % rows * NY + spot // rows == query, 1.0, 0.0).astype(BF16)
-    table = score_own[...]
-    take(scores.at[pl.ds(0, len(everyone))], f_sem.at[1])
-    for pair_to in everyone:
-        table = table + scores[pair_to[0] * 2 + pair_to[1]]
-    high, low = split(table)
-    lowest = (table - high.astype(F32) - low.astype(F32)).astype(BF16)
-    picked = dot(high, onehot, NN) + (dot(low, onehot, NN) + dot(lowest, onehot, NN))
-    out_ref[...] = picked[0:NY, :] * (1.0 / (2 * half * RANK))
+    table = mine
+    take(scores.at[pl.ds(1, 2 * NY - 1)], f_sem.at[1])
+    for change in range(1, 2 * NY):
+        table = table + scores[change]
+    picked = dot(jnp.concatenate(split(table), axis=0), onehot, NN)
+    out_ref[...] = (picked[0:NY, :] + picked[8 : 8 + NY, :]) * (1.0 / (2 * half * RANK))
 
     take(part.at[pl.ds(0, NY // 2)], core_send)
+    take(relayed, relay_send)
     take(gathered, y_send)
     take(sketch_part, swap_sem.at[0])
     take(sketches.at[pl.ds(0, (NZ - 1) * block)], z_send)
     take(sketches.at[pl.ds(0, (NX - 1) * NZ * block)], x_send)
     take(preconds.at[pl.ds(0, (NY - 1) * block)], p_sem.at[0])
-    take(scores.at[pl.ds(0, len(everyone))], f_sem.at[0])
+    take(scores.at[pl.ds(1, 2 * NY - 1)], f_sem.at[0])
 
 
 def local(
@@ -289,7 +312,8 @@
             pltpu.VMEM((2 * NY, query_ids.shape[0] // (2 * NY)), jnp.int32),
             pltpu.VMEM((NY, 2, half, 2 * RANK), F32),
             pltpu.VMEM((NY, half, 2 * RANK), F32),
-            pltpu.VMEM((NY - 1, half, 2 * RANK), F32),
+            pltpu.VMEM((2, half // 2, 2 * RANK), F32),
+            pltpu.VMEM((2, half, 2 * RANK), F32),
             pltpu.VMEM((RANK // 2, 2 * RANK), F32),
             pltpu.VMEM((RANK // 2, 2 * RANK), F32),
             pltpu.VMEM((NX * NZ * RANK // 4, 2 * RANK), F32),
@@ -303,7 +327,9 @@
             dma((NY,)),
             dma((2,)),
             dma(()),
-            dma((NY - 1,)),
+            dma((2,)),
+            dma(()),
+            dma((2,)),
             dma(()),
             dma((NZ,)),
             dma(()),

time: 35.9 us -> 34.8 us (0.969)
  Pallas kernels: 34.5 us -> 33.5 us
    pallas_call x1, Pallas kernels: 34.5 us -> 33.5 us  [local(): pl.pallas_call(kernel, out_shape=jax.ShapeDtypeStruct((NY, query_ids.shap...]
where the time goes in v3:
time: 34.8 us; the launch traced here: 34.7 us
  Pallas kernels  33.5 us (96%)
  local copies, waits for them, and re-layouts  1.26 us (4%)
    pallas_call x1, Pallas kernels, local(): pl.pallas_call(kernel, out_shape=jax.ShapeDtypeStruct((NY, query_ids.shap...  33.5 us
    unnamed x1, local copies, waits for them, and re-layouts  1.26 us

profile of v3, /device:TPU:1, one launch (start us, length us, event | category | flops | bytes accessed | tf_op | source)
XLA Modules:
  0.0 34.7 jit_solution(2141543579705981258)
XLA Ops:
  0.0 33.5 %sketch_scores.1 = f32[4,128]{1,0:T(4,128)} custom-call(bf16[2048,512]{1,0:T(8,128)(2,1)} %act_hbm.1, bf16[2048,1792]{1,0:T(8,128)(2,1)} %grad_hbm.1, bf16[64,512]{1,0:T(8,128)(2,1)} %bitcast.4, bf16[64,1792]{1,0:T(8,128)(2,1)} %bitcast.3, f32[64,64]{1,0:T(8,128)} %left_hbm.1, f32[64,64]{1,0:T(8,128)} %right_hbm.1, s32[4]{0:T(128)} %lengths_hbm.1, ...), custom_call_target="tpu_custom_call" | custom-call | tf_op jit(solution)/shard_map/sketch_scores/pallas_call | solution.py:300
  33.5 1.3 %copy.10 = f32[4,128]{1,0:T(4,128)} copy(f32[4,128]{1,0:T(4,128)} %sketch_scores.1) | data formatting | bytes 4096

commit v4 on v3

--- a/solution.py
+++ b/solution.py
@@ -13,6 +13,7 @@
 ORDER = ((0, 0), (0, 1), (1, 0), (2, 0), (1, 1), (2, 1), (3, 0), (3, 1))
 MERGES = {2: 0, 4: 1, 5: 2}
 WINDOW = 5
+PIECES = 4
 F32 = jnp.float32
 BF16 = jnp.bfloat16
 NN = (((1,), (0,)), ((), ()))
@@ -140,11 +141,13 @@
 
     quarter = half // 2
 
-    def to_relay(up):
-        piece = pl.ds(0 if up else quarter, quarter)
+    size = quarter // PIECES
+
+    def to_relay(up, piece):
+        rows = pl.ds((0 if up else quarter) + piece * size, size)
         return remote(
-            part.at[0, 1, piece], relayed.at[up], relay_send, relay_recv.at[up],
-            device(0, 1 if up else NY - 1, 0, 0),
+            part.at[0, 1, rows], relayed.at[up, pl.ds(piece * size, size)], relay_send,
+            relay_recv.at[up, piece], device(0, 1 if up else NY - 1, 0, 0),
         )
 
     def to_chip(up, first):
@@ -158,23 +161,30 @@
         to_core(step).wait_recv()
         part[step, 1] = part[step, 1] + pair[step]
         if step == 0:
-            to_relay(1).start()
-            to_relay(0).start()
+            for piece in range(PIECES):
+                to_relay(1, piece).start()
+                to_relay(0, piece).start()
         elif step < 3:
             to_chip(2 - step, step == 2).start()
 
-    def relay(up):
-        piece = slice(0, quarter) if up else slice(quarter, half)
-        to_relay(up).wait_recv()
-        part[2 - up, 1, piece] = part[2 - up, 1, piece] + relayed[up]
-        to_chip(up, up == 1).start()
+    def relay(up, piece):
+        start = (0 if up else quarter) + piece * size
+        rows = slice(start, start + size)
+        to_relay(up, piece).wait_recv()
+        part[2 - up, 1, rows] = part[2 - up, 1, rows] + relayed[up, piece * size : (piece + 1) * size]
+        cut = pl.ds(start, size)
+        remote(
+            part.at[2 - up, 1, cut], gathered.at[up, cut], y_send, y_recv.at[up],
+            device(0, 1 if up else NY - 1, 0, 0),
+        ).start()
 
     for index in range(len(ORDER)):
         project(index)
         if index in MERGES:
             merge(MERGES[index])
-    relay(1)
-    relay(0)
+    for piece in range(PIECES):
+        relay(1, piece)
+        relay(0, piece)
     merge(3)
 
     last = len(OFFSETS) - 1
@@ -299,7 +309,7 @@
     dma = pltpu.SemaphoreType.DMA
     return pl.pallas_call(
         kernel,
-        out_shape=jax.ShapeDtypeStruct((NY, query_ids.shape[0] // (2 * NY)), F32),
+        out_shape=pltpu.VMEM((NY, query_ids.shape[0] // (2 * NY)), F32),
         in_specs=[pl.BlockSpec(memory_space=pltpu.HBM)] * 8,
         out_specs=pl.BlockSpec(memory_space=pltpu.VMEM),
         scratch_shapes=[
@@ -327,7 +337,7 @@
             dma((NY,)),
             dma((2,)),
             dma(()),
-            dma((2,)),
+            dma((2, PIECES)),
             dma(()),
             dma((2,)),
             dma(()),
@@ -338,12 +348,17 @@
             dma((2,)),
         ],
         compiler_params=pltpu.CompilerParams(
-            collective_id=0, has_side_effects=True, vmem_limit_bytes=60 * 2**20
+            collective_id=0, has_side_effects=True, vmem_limit_bytes=50 * 2**20
         ),
         name="sketch_scores",
     )(
-        activations, hidden_grads, basis_in.T, basis_out.T, precond_out, precond_in, lengths,
-        query_ids.reshape(2 * NY, -1),
+        *(
+            pltpu.with_memory_space_constraint(array, pltpu.HBM)
+            for array in (
+                activations, hidden_grads, basis_in.T, basis_out.T, precond_out, precond_in,
+                lengths, query_ids.reshape(2 * NY, -1),
+            )
+        )
     )
 
 

time: 34.8 us -> 33.1 us (0.951)
  Pallas kernels: 33.5 us -> 32.4 us
  local copies, waits for them, and re-layouts: 1.26 us -> 0.58 us
    pallas_call x1, Pallas kernels: 33.5 us -> 32.4 us  [local(): pl.pallas_call(kernel, out_shape=pltpu.VMEM((NY, query_ids.shape[0] // (2...]
    unnamed x1, local copies, waits for them, and re-layouts: 1.26 us -> 0.58 us
where the time goes in v4:
time: 33.1 us; the launch traced here: 33 us
  Pallas kernels  32.4 us (98%)
  local copies, waits for them, and re-layouts  0.58 us (2%)
    pallas_call x1, Pallas kernels, local(): pl.pallas_call(kernel, out_shape=pltpu.VMEM((NY, query_ids.shape[0] // (2...  32.4 us

profile of v4, /device:TPU:1, one launch (start us, length us, event | category | flops | bytes accessed | tf_op | source)
XLA Modules:
  0.0 33.0 jit_solution(15730606758614032663)
XLA Ops:
  0.0 32.4 %sketch_scores.1 = f32[4,128]{1,0:T(4,128)S(1)} custom-call(bf16[2048,512]{1,0:T(8,128)(2,1)} %act_hbm.1, bf16[2048,1792]{1,0:T(8,128)(2,1)} %grad_hbm.1, bf16[64,512]{1,0:T(8,128)(2,1)} %bitcast.4, bf16[64,1792]{1,0:T(8,128)(2,1)} %bitcast.3, f32[64,64]{1,0:T(8,128)} %left_hbm.1, f32[64,64]{1,0:T(8,128)} %right_hbm.1, s32[4]{0:T(128)} %lengths_hbm.1, ...), custom_call_target="tpu_custom_call" | custom-call | tf_op jit(solution)/shard_map/sketch_scores/pallas_call | solution.py:310
  32.4 0.6 %copy.10 = f32[4,128]{1,0:T(4,128)} copy(f32[4,128]{1,0:T(4,128)S(1)} %sketch_scores.1) | data formatting | bytes 4096

commit v5 on v4

--- a/solution.py
+++ b/solution.py
@@ -1,3 +1,5 @@
+import functools
+
 import jax
 import jax.numpy as jnp
 from jax import lax
@@ -13,7 +15,9 @@
 ORDER = ((0, 0), (0, 1), (1, 0), (2, 0), (1, 1), (2, 1), (3, 0), (3, 1))
 MERGES = {2: 0, 4: 1, 5: 2}
 WINDOW = 5
+DIRECT = ((0, 0),)
 PIECES = 4
+RELAYS = {6: (0, 1), 7: (2, 3)}
 F32 = jnp.float32
 BF16 = jnp.bfloat16
 NN = (((1,), (0,)), ((), ()))
@@ -43,7 +47,7 @@
     out_ref,
     act, grad, basis, weight, factors, lengths, ids,
     part, pair, relayed, gathered, sketch_part, sketch_pair, sketches, preconds, precond_own, score_own, scores,
-    load_sem, small_sem, core_send, core_recv, swap_sem, relay_send, relay_recv, y_send, y_recv, z_send, z_recv, x_send, x_recv,
+    load_sem, small_sem, core_send, core_recv, swap_sem, relay_send, relay_recv, y_send, y_recv, z_send, z_recv, x_send, x_recv, direct_send,
     p_sem, f_sem,
 ):
     dp = lax.axis_index("dp")
@@ -109,6 +113,22 @@
     for partner in partners:
         pl.semaphore_signal(barrier, 1, device_id=device(*partner), device_id_type=MESH)
 
+    def off_axes(spot):
+        return jnp.logical_and(x != spot[0], z != spot[1])
+
+    def sends_direct(target_x):
+        hits = [jnp.logical_and(target_x == at_x, z == at_z) for at_x, at_z in DIRECT]
+        return functools.reduce(jnp.logical_or, hits)
+
+    @pl.when(sends_direct(x))
+    def _():
+        for dx in range(1, NX):
+            for dz in range(1, NZ):
+                pl.semaphore_signal(
+                    barrier, 1, device_id=device(dx, 0, dz, 0), device_id_type=MESH
+                )
+
+
     load(1)
     basis[0:RANK, act.shape[1] :] = jnp.zeros((RANK, grad.shape[1]), BF16)
     basis[RANK:, 0 : act.shape[1]] = jnp.zeros((RANK, act.shape[1]), BF16)
@@ -130,7 +150,8 @@
         )
         if not mine:
             if index == 0:
-                pl.semaphore_wait(barrier, len(partners))
+                more = sum(off_axes(spot).astype(jnp.int32) for spot in DIRECT)
+                pl.semaphore_wait(barrier, len(partners) + more)
             to_core(step).start()
 
     def to_core(step):
@@ -182,9 +203,9 @@
         project(index)
         if index in MERGES:
             merge(MERGES[index])
-    for piece in range(PIECES):
-        relay(1, piece)
-        relay(0, piece)
+        for piece in RELAYS.get(index, ()):
+            relay(1, piece)
+            relay(0, piece)
     merge(3)
 
     last = len(OFFSETS) - 1
@@ -232,10 +253,17 @@
         spot = place(x, lax.rem(z + NZ - dz, NZ))
         return remote(spot, spot, x_send, x_recv.at[dx], device(dx, 0, 0, 0))
 
+    def to_direct(index):
+        at_x, at_z = DIRECT[index]
+        recv = x_recv.at[lax.rem(at_x + NX - x, NX)]
+        return remote(own, own, direct_send.at[index], recv, (at_x * NZ + at_z, tensor))
+
+    for index, spot in enumerate(DIRECT):
+        pl.when(off_axes(spot))(to_direct(index).start)
+    for dx in others(x, NX):
+        to_x(dx, 0).start()
     for dz in others(z, NZ):
         to_z(dz).start()
-    for dx in others(x, NX):
-        to_x(dx, 0).start()
 
     whole = jnp.concatenate([packed[:, 0:RANK], packed[:, RANK:]], axis=0)
     halfway = dot_split(split(whole), right_split, NN)
@@ -256,7 +284,7 @@
     for dz in Z_ARRIVAL:
         from_z(dz).wait_recv()
         for dx in others(x, NX):
-            to_x(dx, dz).start()
+            pl.when(jnp.logical_not(sends_direct(lax.rem(x + dx, NX))))(to_x(dx, dz).start)
     take(preconds.at[pl.ds(0, (NY - 1) * block)], p_sem.at[1])
     weights = split(
         jnp.concatenate([preconds[pl.ds(row, NY, stride=block), :] for row in range(block)], axis=1)
@@ -295,7 +323,20 @@
     take(gathered, y_send)
     take(sketch_part, swap_sem.at[0])
     take(sketches.at[pl.ds(0, (NZ - 1) * block)], z_send)
-    take(sketches.at[pl.ds(0, (NX - 1) * NZ * block)], x_send)
+    skips = sum(sends_direct(lax.rem(x + dx, NX)).astype(jnp.int32) for dx in range(1, NX))
+    for count in range(NX):
+
+        @pl.when(skips == count)
+        def _():
+            blocks = (NX - 1) * NZ - count * (NZ - 1)
+            take(sketches.at[pl.ds(0, blocks * block)], x_send)
+
+    for index, spot in enumerate(DIRECT):
+
+        @pl.when(off_axes(spot))
+        def _():
+            take(sketches.at[pl.ds(0, block)], direct_send.at[index])
+
     take(preconds.at[pl.ds(0, (NY - 1) * block)], p_sem.at[0])
     take(scores.at[pl.ds(1, 2 * NY - 1)], f_sem.at[0])
 
@@ -344,6 +385,7 @@
             dma((NZ,)),
             dma(()),
             dma((NX,)),
+            dma((len(DIRECT),)),
             dma((2,)),
             dma((2,)),
         ],

time: 33.1 us -> 31.6 us (0.955)
  the two profiles are of different devices: /device:TPU:1 before, /device:TPU:33 now
where the time goes in v5:
time: 31.6 us
  Pallas kernels  31 us (98%)
  local copies, waits for them, and re-layouts  0.58 us (2%)
    pallas_call x1, Pallas kernels, local(): pl.pallas_call(kernel, out_shape=pltpu.VMEM((NY, query_ids.shape[0] // (2...  31 us

profile of v5, /device:TPU:33, one launch (start us, length us, event | category | flops | bytes accessed | tf_op | source)
XLA Modules:
  0.0 31.6 jit_solution(14252046415098284936)
XLA Ops:
  0.0 31.0 %sketch_scores.1 = f32[4,128]{1,0:T(4,128)S(1)} custom-call(bf16[2048,512]{1,0:T(8,128)(2,1)} %act_hbm.1, bf16[2048,1792]{1,0:T(8,128)(2,1)} %grad_hbm.1, bf16[64,512]{1,0:T(8,128)(2,1)} %bitcast.4, bf16[64,1792]{1,0:T(8,128)(2,1)} %bitcast.3, f32[64,64]{1,0:T(8,128)} %left_hbm.1, f32[64,64]{1,0:T(8,128)} %right_hbm.1, s32[4]{0:T(128)} %lengths_hbm.1, ...), custom_call_target="tpu_custom_call" | custom-call | tf_op jit(solution)/shard_map/sketch_scores/pallas_call | solution.py:351
  31.0 0.6 %copy.10 = f32[4,128]{1,0:T(4,128)} copy(f32[4,128]{1,0:T(4,128)S(1)} %sketch_scores.1) | data formatting | bytes 4096

commit v6 on v5

--- a/solution.py
+++ b/solution.py
@@ -14,7 +14,7 @@
 Z_ARRIVAL = (1, 7, 2, 6, 3, 5, 4)
 ORDER = ((0, 0), (0, 1), (1, 0), (2, 0), (1, 1), (2, 1), (3, 0), (3, 1))
 MERGES = {2: 0, 4: 1, 5: 2}
-WINDOW = 5
+WINDOW = 3
 DIRECT = ((0, 0),)
 PIECES = 4
 RELAYS = {6: (0, 1), 7: (2, 3)}
@@ -102,9 +102,9 @@
         pltpu.make_async_copy(act_hbm.at[rows], act.at[slot], load_sem.at[index]).start()
         pltpu.make_async_copy(grad_hbm.at[rows], grad.at[slot], load_sem.at[index]).start()
 
+    load(0)
     small[0].start()
     small[1].start()
-    load(0)
 
     barrier = pltpu.get_barrier_semaphore()
     partners = [(0, dy, 0, flip) for dy in range(NY) for flip in (0, 1) if dy or flip]
@@ -306,7 +306,7 @@
         target = lax.rem(tensor + change, 2 * NY)
         return remote(score_own, scores.at[change], f_sem.at[0], f_sem.at[1], (dp, target))
 
-    for change in others(tensor, 2 * NY):
+    for change in (4, 5, 3, 2, 6, 7, 1):
         exchange(change).start()
     query = ids[pl.ds(tensor, 1), :]
     spot = lax.broadcasted_iota(jnp.int32, (rows * NY, rows * NY), 0)

time: 31.6 us -> 31.1 us (0.984)
  the two profiles are of different devices: /device:TPU:33 before, /device:TPU:2 now
where the time goes in v6:
time: 31.1 us; the launch traced here: 31 us
  Pallas kernels  30.4 us (98%)
  local copies, waits for them, and re-layouts  0.58 us (2%)
    pallas_call x1, Pallas kernels, local(): pl.pallas_call(kernel, out_shape=pltpu.VMEM((NY, query_ids.shape[0] // (2...  30.4 us

profile of v6, /device:TPU:2, one launch (start us, length us, event | category | flops | bytes accessed | tf_op | source)
XLA Modules:
  0.0 31.0 jit_solution(15458849775182899845)
XLA Ops:
  0.0 30.4 %sketch_scores.1 = f32[4,128]{1,0:T(4,128)S(1)} custom-call(bf16[2048,512]{1,0:T(8,128)(2,1)} %act_hbm.1, bf16[2048,1792]{1,0:T(8,128)(2,1)} %grad_hbm.1, bf16[64,512]{1,0:T(8,128)(2,1)} %bitcast.4, bf16[64,1792]{1,0:T(8,128)(2,1)} %bitcast.3, f32[64,64]{1,0:T(8,128)} %left_hbm.1, f32[64,64]{1,0:T(8,128)} %right_hbm.1, s32[4]{0:T(128)} %lengths_hbm.1, ...), custom_call_target="tpu_custom_call" | custom-call | tf_op jit(solution)/shard_map/sketch_scores/pallas_call | solution.py:351
  30.4 0.6 %copy.10 = f32[4,128]{1,0:T(4,128)} copy(f32[4,128]{1,0:T(4,128)S(1)} %sketch_scores.1) | data formatting | bytes 4096
